TPU v7x, 128 devices: a whole 4x4x4 slice. The times are simulated.
128 devices in a mesh: dp: 16 (over z, y), tensor: 8 (over x, core).
Axes of the slice: x: 4, y: 4, z: 4, core: 2. Of those that a mesh axis runs over, the one named last changes fastest.
Arguments:
- tile_tokens: bfloat16 [256, 256, 1536], P('dp'), may hold values from -6 to 6
- vit_qkv: bfloat16 [1536, 24, 3, 64], P(None, 'tensor'), as said below
- vit_out: bfloat16 [1536, 1536], P('tensor'), may hold values from -0.15625 to 0.15625
- tile_norm_gain: bfloat16 [1536], replicated, may hold values from 0.099609375 to 1.8984375
- fresh_proj: bfloat16 [1536, 768], replicated, may hold values from -0.15625 to 0.15625
- tile_target: int32 [256], replicated, may hold values from 0 to 16383
- cached_rows: bfloat16 [16384, 768], P(('dp', 'tensor')), may hold values from -6 to 6
- slide_tiles: int32 [4], replicated, may hold values from 1 to 8192, 16384 in all
- head_shift: int32 [16], replicated, may hold values from 0 to 15
- long_gain: bfloat16 [768], replicated, may hold values from 0.099609375 to 1.8984375
- long_qkv: bfloat16 [768, 16, 3, 48], replicated, as said below
- long_out: bfloat16 [768, 768], replicated, may hold values from -0.21875 to 0.21875
Outputs:
- slide_output: bfloat16 [16384, 768], P(('dp', 'tensor'))
Inputs may be any that keep to these rules, and one draw needn't show every extreme that they name: `slide_tiles`: the counts sum to 16384; the largest is exactly 8192. `tile_target`: rows may repeat. `vit_qkv`: dense projection entries. `long_qkv`: dense projection entries.
All inputs are finite; a program needn't handle non-finite values.
Results may differ from a plain program's by a relative error of at most 0.006.
Values may be sent and summed in bfloat16 or wider, within the bound.
A program may use at most 192 MiB of HBM per device.

v0:
```python
import functools
import math

import jax
import jax.numpy as jnp
from jax import lax
from jax.experimental import pallas as pl
from jax.experimental.pallas import tpu as pltpu
from jax.sharding import PartitionSpec as P

MESH = pl.DeviceIdType.MESH
EPSILON = 1e-06
OUTSIDE = -1e30
LOG2E = 1.4426950408889634
NN = (((1,), (0,)), ((), ()))
NT = (((1,), (1,)), ((), ()))
TN = (((0,), (0,)), ((), ()))
F32 = jnp.float32
BF16 = jnp.bfloat16

TILES_HERE = 16
TOK = 256
D = 1536
VH_HERE = 3
VS = 64
VW = VH_HERE * 3 * VS
LD = 768
LH = 16
LS = 48
LW = 3 * LS
ROWS = 128
SEG = 1024
CHUNK = 2048
KX = 64
GROUP = 2
WIDE = GROUP * TOK
AHEAD = 4
VIT_SCALE = LOG2E / math.sqrt(VS)
LONG_SCALE = LOG2E / math.sqrt(LS)


def dot(a, b, dims=NN):
    return lax.dot_general(a, b, dims, preferred_element_type=F32)


def iota(shape, dim):
    return lax.broadcasted_iota(jnp.int32, shape, dim)


def split3(value):
    high = value.astype(BF16)
    rest = value - high.astype(F32)
    middle = rest.astype(BF16)
    low = (rest - middle.astype(F32)).astype(BF16)
    return high, middle, low


def normalize_rows(values):
    center = values - jnp.mean(values, axis=-1, keepdims=True)
    return center * lax.rsqrt(jnp.mean(center * center, axis=-1, keepdims=True) + EPSILON)


def whole_row(ref):
    rows = ref[...].astype(F32)
    return jnp.concatenate([rows[k : k + 1] for k in range(rows.shape[0])], axis=1)


def bit_reversed(rank):
    return (rank % 2) * 8 + (rank // 2 % 2) * 4 + (rank // 4 % 2) * 2 + rank // 8


def whole_kernel(
    tokens_hbm,
    vit_qkv_hbm,
    vit_out_hbm,
    tile_gain_ref,
    fresh_proj_hbm,
    target_ref,
    cached_hbm,
    slide_tiles_ref,
    head_shift_ref,
    long_gain_ref,
    long_qkv_hbm,
    long_out_hbm,
    out_ref,
    tokens,
    vit_qkv,
    csum,
    projected,
    attended,
    token_mean,
    vit_out,
    fresh_proj,
    cached,
    long_qkv,
    long_out,
    part,
    part_in,
    fresh_in,
    fresh_all,
    hidden,
    named_out,
    named_in,
    named_mid,
    named_all,
    same,
    lands,
    keep,
    packed,
    qkv,
    perm,
    qx,
    kx,
    vx,
    keys_by_row,
    send2,
    send3,
    send4,
    got2,
    got3,
    got4,
    num,
    top,
    mix_out,
    mix_in,
    token_sem,
    load_sem,
    sems,
):
    d = lax.axis_index("dp")
    t = lax.axis_index("tensor")
    chunk = d // 2
    half = d % 2
    mine = half * 8 + t

    def remote(i, src, dst, device):
        return pltpu.make_async_remote_copy(
            src_ref=src,
            dst_ref=dst,
            send_sem=sems.at[0, i],
            recv_sem=sems.at[1, i],
            device_id=device,
            device_id_type=MESH,
        )

    def tile_rows(index):
        return pl.ds(pl.multiple_of(index * 16, 16), 16)

    def chunk_device(index):
        return 2 * chunk + index // 8, index % 8

    def named_copy(k):
        peer = (d + k) % 16
        return remote(
            k - 1, named_out.at[tile_rows(peer)], named_in.at[tile_rows(d)], (peer, t)
        )

    def middle_copy(k):
        slot = named_mid.at[tile_rows(t)]
        return remote(14 + k, slot, slot, (d, (t + k) % 8))

    def last_copy(k):
        slot = named_all.at[tile_rows(d)]
        return remote(21 + k, slot, slot, ((d + k) % 16, t))

    def head_copy(k):
        lanes = pl.ds(pl.multiple_of(mine * ROWS, ROWS), ROWS)
        return remote(
            36 + k, packed.at[k - 1], qkv.at[:, lanes], chunk_device((mine + k) % 16)
        )

    def far_copy(k):
        quad, inner = chunk // 4, chunk % 4
        if k == 0:
            return remote(52, send2, got2, (2 * (chunk + 1 - 2 * (chunk % 2)) + half, t))
        if k < 3:
            other = quad * 4 + (1 - inner // 2) * 2 + (inner % 2 + k - 1) % 2
            return remote(52 + k, send3, got3.at[k - 1], (2 * other + half, t))
        other = (1 - quad) * 4 + (inner + k - 3) % 4
        return remote(52 + k, send4, got4.at[k - 3], (2 * other + half, t))

    def reduce_copy(k):
        peer = (t + k) % 8
        return remote(58 + k, part.at[peer], part_in.at[t], (d, peer))

    def gather_copy(k):
        return remote(65 + k, fresh_in.at[t], fresh_in.at[t], (d, (t + k) % 8))

    def spread_copy(k):
        slot = fresh_all.at[tile_rows(d)]
        return remote(72 + k, slot, slot, ((d + k) % 16, t))

    def mix_copy(k):
        device = (mine + k) % 16
        return remote(87 + k, mix_out.at[device], mix_in.at[mine], chunk_device(device))

    def every(copy, count, what):
        first = 0 if copy is far_copy else 1
        for k in range(first, first + count):
            getattr(copy(k), what)()

    barrier = pltpu.get_barrier_semaphore()
    for k in range(1, 8):
        pl.semaphore_signal(barrier, 1, device_id=(d, (t + k) % 8), device_id_type=MESH)
        pl.semaphore_signal(
            barrier, 1, device_id=(2 * chunk + 1 - half, (t + k) % 8), device_id_type=MESH
        )
    for k in range(1, 16):
        pl.semaphore_signal(barrier, 1, device_id=((d + k) % 16, t), device_id_type=MESH)

    vit_load = pltpu.make_async_copy(vit_qkv_hbm, vit_qkv.at[0:VW], load_sem.at[5])
    vit_load.start()
    loads = [
        pltpu.make_async_copy(src, dst, load_sem.at[i])
        for i, (src, dst) in enumerate(
            [
                (vit_out_hbm, vit_out),
                (fresh_proj_hbm, fresh_proj),
                (cached_hbm, cached),
                (long_qkv_hbm, long_qkv),
                (long_out_hbm, long_out),
            ]
        )
    ]
    loads[2].start()
    def token_load(i):
        return pltpu.make_async_copy(tokens_hbm.at[i], tokens.at[i], token_sem.at[i])

    for i in range(AHEAD):
        token_load(i).start()
    loads[3].start()

    row = iota((16, D), 0)
    col = iota((16, D), 1)
    extra = jnp.where(row == 0, 1.0, jnp.where((row == 1) & (col == 0), 1.0, 0.0))
    vit_qkv[VW : VW + 16, :] = extra.astype(BF16)
    shift = head_shift_ref[mine] % 16
    place = iota((SEG, 1), 0)
    goal = bit_reversed((place + 16 - shift) % 16) * 64 + place // 16
    perm[...] = jnp.where(goal == iota((SEG, SEG), 1), 1.0, 0.0).astype(BF16)
    end0 = slide_tiles_ref[0]
    end1 = end0 + slide_tiles_ref[1]
    end2 = end1 + slide_tiles_ref[2]

    def slides(count, width, which):
        lane = iota((16, count), 1)
        spot = lane % width
        row = (
            SEG * (2 * which + lane // width)
            + 16 * (spot % 64)
            + (bit_reversed(spot // 64) + shift) % 16
        )
        return (
            (row >= end0).astype(jnp.int32)
            + (row >= end1).astype(jnp.int32)
            + (row >= end2).astype(jnp.int32)
        )

    def query_marks(count, width, which):
        ids = slides(count, width, which)
        return jnp.where(ids == iota(ids.shape, 0), 1.0, 0.0).astype(BF16)

    def key_marks(count, width, which):
        ids = slides(count, width, which)
        feature = iota(ids.shape, 0)
        return jnp.where((feature < 4) & (ids != feature), OUTSIDE, 0.0).astype(BF16)

    def value_marks(count):
        return jnp.where(iota((16, count), 0) == 0, 1.0, 0.0).astype(BF16)

    qx[LS:KX, :] = query_marks(CHUNK, SEG, chunk)
    kx[LS:KX, :] = key_marks(CHUNK, SEG, chunk)
    vx[LS:KX, :] = value_marks(CHUNK)


    lane_target = target_ref[...]
    diagonal = iota((256, 256), 0) == iota((256, 256), 1)
    target = jnp.sum(
        jnp.where(diagonal, lane_target.astype(F32), 0.0), axis=1, keepdims=True
    ).astype(jnp.int32)
    equal = target == lane_target
    same[...] = jnp.where(equal, 1.0, 0.0).astype(BF16)
    earlier = jnp.where(equal & (iota((256, 256), 1) < iota((256, 256), 0)), 1.0, 0.0)
    leads = jnp.sum(earlier, axis=1, keepdims=True) < 0.5

    def landing(which, width):
        away = target - which * CHUNK
        spot = away % SEG
        lane = bit_reversed((spot + 16 - shift) % 16) * 64 + spot // 16
        good = leads & (away >= 0) & (away < CHUNK) & (lane < width)
        goal = jnp.where(good, away // SEG * width + lane, -1)
        return jnp.where(goal == iota((256, 2 * width), 1), 1.0, 0.0).astype(BF16)

    quad = chunk // 4
    inner = chunk % 4
    beside = chunk + 1 - 2 * (chunk % 2)
    across = [quad * 4 + (1 - inner // 2) * 2 + (inner % 2 + k) % 2 for k in range(2)]
    beyond = [(1 - quad) * 4 + (inner + 4 - k) % 4 for k in range(4)]
    lands[:, 0:CHUNK] = landing(chunk, SEG)
    lands[:, CHUNK : CHUNK + 512] = landing(beside, 256)
    for k in range(2):
        begin = CHUNK + 512 + 256 * k
        lands[:, begin : begin + 256] = landing(across[k], 128)
    for k in range(4):
        begin = CHUNK + 1024 + 128 * k
        lands[:, begin : begin + 128] = landing(beyond[k], 64)
    keep[...] = 1.0 - dot(jnp.ones((16, 256), BF16), lands[:, 0:CHUNK])[0:8]

    loads[2].wait()
    first_row = (d * 8 + t) * ROWS
    stored = cached[...]
    hidden[...] = (normalize_rows(stored.astype(F32)) * whole_row(long_gain_ref)).astype(BF16)
    mine_only = jnp.where(target - first_row == iota((256, ROWS), 1), 1.0, 0.0).astype(BF16)
    named_out[...] = dot(mine_only, stored).astype(BF16)
    pl.semaphore_wait(barrier, 29)
    every(named_copy, 15, "start")
    named_in[tile_rows(d)] = named_out[tile_rows(d)]

    def sum_over_dp():
        every(named_copy, 15, "wait_recv")
        total = sum(named_in[16 * k : 16 * k + 16].astype(F32) for k in range(16))
        named_mid[tile_rows(t)] = total.astype(BF16)
        every(middle_copy, 7, "start")

    def sum_over_tensor():
        every(middle_copy, 7, "wait_recv")
        total = sum(named_mid[16 * k : 16 * k + 16].astype(F32) for k in range(8))
        named_all[tile_rows(d)] = total.astype(BF16)
        every(last_copy, 15, "start")

    def head_block(head):
        weight = long_qkv[pl.ds(pl.multiple_of(head * LW, LW), LW), :]
        return dot(weight, hidden[...], NT).astype(BF16)

    def send_heads():
        loads[3].wait()

        def send_head(k, carry):
            packed[k - 1] = head_block((mine + k) % 16)
            head_copy(k).start()
            return carry

        lax.fori_loop(1, 16, send_head, 0)
        qkv[:, pl.ds(pl.multiple_of(mine * ROWS, ROWS), ROWS)] = head_block(mine)

    def sort_rows():
        every(head_copy, 15, "wait_recv")
        low_half = iota((LW, 128), 1) < 64
        sides = []
        for side in range(2):
            lanes = slice(side * SEG, (side + 1) * SEG)
            ordered = dot(qkv[:, lanes], perm[...]) * keep[0:1, lanes]
            sides.append(ordered[:, 0:128])
            ordered = ordered.astype(BF16)
            qx[0:LS, lanes] = ordered[0:LS]
            kx[0:LS, lanes] = ordered[LS : 2 * LS]
            vx[0:LS, lanes] = ordered[2 * LS : LW]
            send2[:, side * 256 : (side + 1) * 256] = ordered[LS:LW, 0:256]
            send3[:, side * 128 : (side + 1) * 128] = ordered[LS:LW, 0:128]
        both = jnp.where(low_half, sides[0], pltpu.roll(sides[1], 64, 1)).astype(BF16)
        send4[...] = both[LS:LW]
        every(far_copy, 7, "start")

    vit_load.wait()
    csum[...] = dot(vit_qkv[0:VW], jnp.ones((D, 128), BF16))

    def project(group):
        for i in range(GROUP):
            token_load(group * GROUP + i).wait()
        for i in range(GROUP):
            after = group * GROUP + i + AHEAD

            @pl.when(after < TILES_HERE)
            def _():
                token_load(after).start()

        x = tokens[pl.ds(group * GROUP, GROUP)].reshape(WIDE, D)
        raw = dot(vit_qkv[...], x, NT)
        mean = raw[VW : VW + 1] * (1.0 / D)
        shift_row = mean - raw[VW + 1 : VW + 2]
        first = x[:, 0:1].astype(F32)
        squares = jnp.zeros((WIDE, 128), F32)
        for k in range(D // 128):
            delta = x[:, 128 * k : 128 * (k + 1)].astype(F32) - first
            squares = squares + delta * delta
        ones = jnp.ones((16, 128), BF16)
        total = sum(dot(ones, piece, NT) for piece in split3(squares))
        variance = jnp.maximum(total[0:1] * (1.0 / D) - shift_row * shift_row, 0.0)
        scale = lax.rsqrt(variance + EPSILON)
        spread = jnp.concatenate([csum[...]] * (WIDE // 128), axis=1)
        projected[...] = ((raw[0:VW] - spread * mean) * scale).astype(BF16)

    def attention(group):
        def piece(job, which):
            i, head = job
            first = (head * 3 + which) * VS
            return projected[first : first + VS, i * TOK : (i + 1) * TOK]

        jobs = [(i, head) for i in range(GROUP) for head in range(VH_HERE)]
        scores = [dot(piece(job, 1), piece(job, 0), TN) for job in jobs]
        highest = [jnp.max(score, axis=0, keepdims=True) for score in scores]
        weights = [
            jnp.exp2((score - high) * VIT_SCALE) for score, high in zip(scores, highest)
        ]
        sums = [jnp.sum(weight, axis=0, keepdims=True) for weight in weights]
        mixed = [dot(piece(job, 2), weight.astype(BF16)) for job, weight in zip(jobs, weights)]
        for (i, head), mixture, total in zip(jobs, mixed, sums):
            place = pl.ds(pl.multiple_of((group * GROUP + i) * TOK, TOK), TOK)
            attended[head * VS : (head + 1) * VS, place] = (mixture / total).astype(BF16)

    groups = TILES_HERE // GROUP

    def one_group(group, carry):
        project(group)
        attention(group)

        @pl.when(group == 0)
        def _():
            send_heads()

        @pl.when(group == 1)
        def _():
            sum_over_dp()

        @pl.when(group == 2)
        def _():
            sort_rows()

        @pl.when(group == 3)
        def _():
            sum_over_tensor()
            for i in (0, 1, 4):
                loads[i].start()

        return carry

    lax.fori_loop(0, groups, one_group, 0)
    for i in range(2):
        sums = dot(jnp.ones((16, TOK), BF16), tokens[2 * t + i])
        token_mean[i : i + 1, :] = sums[0:1] * (1.0 / TOK)
    tile_of = iota((TILES_HERE, TILES_HERE * TOK), 1) // TOK
    picks = jnp.where(iota(tile_of.shape, 0) == tile_of, 1.0 / TOK, 0.0).astype(BF16)
    pooled_term = dot(picks, attended[...], NT)

    loads[0].wait()
    high, middle, low = split3(pooled_term)
    weight = vit_out[...]
    partial = dot(high, weight) + dot(middle, weight) + dot(low, weight)
    for k in range(8):
        part[k] = partial[2 * k : 2 * k + 2]
    every(reduce_copy, 7, "start")
    part_in[pl.ds(t, 1)] = part[pl.ds(t, 1)]

    every(reduce_copy, 7, "wait_recv")
    pooled = token_mean[0:2, :]
    for k in range(8):
        pooled = pooled + part_in[k]
    normed = (normalize_rows(pooled) * whole_row(tile_gain_ref)).astype(BF16)
    loads[1].wait()
    fresh = dot(normed, fresh_proj[...])
    fresh_in[pl.ds(t, 1)] = fresh[None]
    every(gather_copy, 7, "start")
    every(gather_copy, 7, "wait_recv")
    group = jnp.concatenate([fresh_in[k] for k in range(8)], axis=0).astype(BF16)
    fresh_all[tile_rows(d)] = group
    every(spread_copy, 15, "start")
    every(last_copy, 15, "wait_recv")
    every(far_copy, 7, "wait_recv")
    every(spread_copy, 15, "wait_recv")

    changed = named_all[...].astype(F32) + dot(same[...], fresh_all[...])
    changed = (normalize_rows(changed) * whole_row(long_gain_ref)).astype(BF16)
    weight = long_qkv[pl.ds(pl.multiple_of(mine * LW, LW), LW), :]
    renewed = dot(weight, changed, NT).astype(BF16)

    def add(ref, rows, lanes, change):
        ref[rows, lanes] = (ref[rows, lanes].astype(F32) + change).astype(BF16)

    change = dot(renewed, lands[:, 0:CHUNK])
    everything = slice(0, CHUNK)
    add(qx, slice(0, LS), everything, change[0:LS])
    add(kx, slice(0, LS), everything, change[LS : 2 * LS])
    add(vx, slice(0, LS), everything, change[2 * LS : LW])
    far_change = dot(renewed[LS:LW], lands[:, CHUNK : CHUNK + 1536])
    for side in range(2):
        lanes = slice(side * SEG, (side + 1) * SEG)
        keys_by_row[lanes, :] = jnp.transpose(kx[:, lanes])

    def attend(keys, values, queries):
        scores = dot(keys, queries)
        highest = jnp.max(scores, axis=0, keepdims=True)
        weights = jnp.exp2((scores - highest) * LONG_SCALE).astype(BF16)
        return dot(values, weights), highest

    def merge(lanes, other_num, other_top):
        old_top = top[0:1, lanes]
        new_top = jnp.maximum(old_top, other_top)
        num[:, lanes] = num[:, lanes] * jnp.exp2(
            (old_top - new_top) * LONG_SCALE
        ) + other_num * jnp.exp2((other_top - new_top) * LONG_SCALE)
        top[0:1, lanes] = new_top

    def first_pair(i, carry):
        for side in range(2):
            lanes = slice(side * SEG, (side + 1) * SEG)
            spot = pl.ds(pl.multiple_of(side * SEG + i * 256, 256), 256)
            result, highest = attend(keys_by_row[lanes, :], vx[:, lanes], qx[:, spot])
            num[:, spot] = result
            top[0:1, spot] = highest
        return carry

    lax.fori_loop(0, 4, first_pair, 0)

    def joined(ref, width):
        return jnp.concatenate([ref[:, 0:width], ref[:, SEG : SEG + width]], axis=1)

    def joined_rows(width):
        return [keys_by_row[0:width, :], keys_by_row[SEG : SEG + width, :]]

    def second_pair(i, carry):
        keys = jnp.concatenate(joined_rows(512), axis=0)
        values = joined(vx, 512)
        for side in range(2):
            spot = pl.ds(pl.multiple_of(side * SEG + i * 256, 256), 256)
            merge(spot, *attend(keys, values, qx[:, spot]))
        return carry

    lax.fori_loop(0, 2, second_pair, 0)

    def arrived(block, begin, count, width, which):
        block = (block.astype(F32) + far_change[:, begin : begin + count]).astype(BF16)
        key = jnp.concatenate([block[0:LS], key_marks(count, width, which)], axis=0)
        value = jnp.concatenate([block[LS : 2 * LS], value_marks(count)], axis=0)
        return jnp.transpose(key), value

    key2, value2 = arrived(got2[...], 0, 512, 256, beside)
    keys = jnp.concatenate(joined_rows(256) + [key2], axis=0)
    values = jnp.concatenate([joined(vx, 256), value2], axis=1)
    for side in range(2):
        lanes = slice(side * SEG, side * SEG + 256)
        merge(lanes, *attend(keys, values, qx[:, lanes]))

    keys3 = joined_rows(128) + [key2[0:128], key2[256:384]]
    values3 = [joined(vx, 128), value2[:, 0:128], value2[:, 256:384]]
    for k in range(2):
        key, value = arrived(got3[k], 512 + 256 * k, 256, 128, across[k])
        keys3 += [key[0:128], key[128:256]]
        values3.append(value)
    keys = jnp.concatenate(keys3, axis=0)
    values = jnp.concatenate(values3, axis=1)
    result, highest = attend(keys, values, joined(qx, 128))
    merge(slice(0, 128), result[:, 0:128], highest[:, 0:128])
    merge(slice(SEG, SEG + 128), result[:, 128:256], highest[:, 128:256])

    lower = iota((KX, 128), 1) < 64

    def packed_pair(a, b):
        moved = pltpu.roll(b.astype(F32), 64, 1)
        return jnp.where(lower, a.astype(F32), moved).astype(BF16)

    keys4 = [key[0:64] for key in keys3]
    own = values3[0]
    values4 = [
        packed_pair(own[:, 0:128], own[:, 128:256]),
        packed_pair(values3[1], values3[2]),
    ]
    for far in values3[3:]:
        values4.append(packed_pair(far[:, 0:128], far[:, 128:256]))
    for k in range(4):
        key, value = arrived(got4[k], 1024 + 128 * k, 128, 64, beyond[k])
        keys4.append(key)
        values4.append(value)
    keys = jnp.concatenate(keys4, axis=0)
    values = jnp.concatenate(values4, axis=1)
    query = packed_pair(qx[:, 0:128], qx[:, SEG : SEG + 128])
    result, highest = attend(keys, values, query)
    highest = jnp.broadcast_to(highest, (8, 128))
    for side in range(2):
        if side == 1:
            result = pltpu.roll(result, 64, 1)
            highest = pltpu.roll(highest, 64, 1)
        lanes = slice(side * SEG, side * SEG + 128)
        merge(
            lanes,
            jnp.where(lower, result, 0.0),
            jnp.where(lower[0:1], highest[0:1], OUTSIDE),
        )

    for side in range(2):
        lanes = slice(side * SEG, (side + 1) * SEG)
        blended = (num[0:LS, lanes] / num[LS : LS + 1, lanes]).astype(BF16)
        natural = dot(blended, perm[...], NT).astype(BF16)
        for i in range(8):
            mix_out[side * 8 + i] = natural[:, i * ROWS : (i + 1) * ROWS]
    every(mix_copy, 15, "start")
    mix_in[pl.ds(mine, 1)] = mix_out[pl.ds(mine, 1)]
    match = (lane_target - first_row == iota((ROWS, 256), 0))
    match = jnp.where(match, 1.0, 0.0).astype(BF16)
    rows = cached[...].astype(F32) + dot(match, fresh_all[...])
    loads[4].wait()
    every(mix_copy, 15, "wait_recv")
    mixture = mix_in[...].reshape(LD, ROWS)
    out_ref[...] = (rows + dot(mixture, long_out[...], TN)).astype(BF16)

    for copy, count in (
        (named_copy, 15),
        (middle_copy, 7),
        (last_copy, 15),
        (head_copy, 15),
        (far_copy, 7),
        (reduce_copy, 7),
        (gather_copy, 7),
        (spread_copy, 15),
        (mix_copy, 15),
    ):
        every(copy, count, "wait_send")


def whole_layer(*arguments):
    vmem = pl.BlockSpec(memory_space=pltpu.VMEM)
    smem = pl.BlockSpec(memory_space=pltpu.SMEM)
    hbm = pl.BlockSpec(memory_space=pl.ANY)
    return pl.pallas_call(
        whole_kernel,
        out_shape=jax.ShapeDtypeStruct((ROWS, LD), BF16),
        in_specs=[hbm, hbm, hbm, vmem, hbm, vmem, hbm, smem, smem, vmem, hbm, hbm],
        out_specs=vmem,
        scratch_shapes=[
            pltpu.VMEM((TILES_HERE, TOK, D), BF16),
            pltpu.VMEM((VW + 16, D), BF16),
            pltpu.VMEM((VW, 128), F32),
            pltpu.VMEM((VW, WIDE), BF16),
            pltpu.VMEM((VH_HERE * VS, TILES_HERE * TOK), BF16),
            pltpu.VMEM((8, D), F32),
            pltpu.VMEM((VH_HERE * VS, D), BF16),
            pltpu.VMEM((D, LD), BF16),
            pltpu.VMEM((ROWS, LD), BF16),
            pltpu.VMEM((LH * LW, LD), BF16),
            pltpu.VMEM((LD, LD), BF16),
            pltpu.VMEM((8, 2, D), F32),
            pltpu.VMEM((8, 2, D), F32),
            pltpu.VMEM((8, 2, LD), F32),
            pltpu.VMEM((256, LD), BF16),
            pltpu.VMEM((ROWS, LD), BF16),
            pltpu.VMEM((256, LD), BF16),
            pltpu.VMEM((256, LD), BF16),
            pltpu.VMEM((128, LD), BF16),
            pltpu.VMEM((256, LD), BF16),
            pltpu.VMEM((256, 256), BF16),
            pltpu.VMEM((256, CHUNK + 1536), BF16),
            pltpu.VMEM((8, CHUNK), F32),
            pltpu.VMEM((15, LW, ROWS), BF16),
            pltpu.VMEM((LW, CHUNK), BF16),
            pltpu.VMEM((SEG, SEG), BF16),
            pltpu.VMEM((KX, CHUNK), BF16),
            pltpu.VMEM((KX, CHUNK), BF16),
            pltpu.VMEM((KX, CHUNK), BF16),
            pltpu.VMEM((CHUNK, KX), BF16),
            pltpu.VMEM((2 * LS, 512), BF16),
            pltpu.VMEM((2 * LS, 256), BF16),
            pltpu.VMEM((2 * LS, 128), BF16),
            pltpu.VMEM((2 * LS, 512), BF16),
            pltpu.VMEM((2, 2 * LS, 256), BF16),
            pltpu.VMEM((4, 2 * LS, 128), BF16),
            pltpu.VMEM((KX, CHUNK), F32),
            pltpu.VMEM((8, CHUNK), F32),
            pltpu.VMEM((16, LS, ROWS), BF16),
            pltpu.VMEM((16, LS, ROWS), BF16),
            pltpu.SemaphoreType.DMA((TILES_HERE,)),
            pltpu.SemaphoreType.DMA((6,)),
            pltpu.SemaphoreType.DMA((2, 103)),
        ],
        compiler_params=pltpu.CompilerParams(
            collective_id=0,
            has_side_effects=True,
            vmem_limit_bytes=60 * 1024 * 1024,
        ),
    )(*arguments)


def body(
    tile_tokens,
    vit_qkv,
    vit_out,
    tile_norm_gain,
    fresh_proj,
    tile_target,
    cached_rows,
    slide_tiles,
    head_shift,
    long_gain,
    long_qkv,
    long_out,
):
    vit_rows = jnp.transpose(vit_qkv, (1, 2, 3, 0)).reshape(VW, D)
    long_rows = jnp.transpose(long_qkv, (1, 2, 3, 0)).reshape(LH * LW, LD)
    return whole_layer(
        tile_tokens,
        vit_rows,
        vit_out,
        tile_norm_gain.reshape(D // 128, 128),
        fresh_proj,
        tile_target.reshape(1, 256),
        cached_rows,
        slide_tiles,
        head_shift,
        long_gain.reshape(LD // 128, 128),
        long_rows,
        long_out,
    )


def solution(mesh):
    placed = (
        P("dp", None, None),
        P(None, "tensor", None, None),
        P("tensor", None),
        P(),
        P(),
        P(),
        P(("dp", "tensor"), None),
        P(),
        P(),
        P(),
        P(),
        P(),
    )
    return jax.shard_map(
        body, mesh=mesh, in_specs=placed, out_specs=P(("dp", "tensor"), None), check_vma=False
    )
```

profile of v0, /device:TPU:1, one launch (start us, length us, event | category | flops | bytes accessed | tf_op | source)
XLA Modules:
  0.0 80.6 jit_solution(11934089432213793728)
XLA Ops:
  0.0 79.0 %shard_map.118 = bf16[128,768]{1,0:T(8,128)(2,1)} custom-call(bf16[16,256,1536]{2,1,0:T(8,128)(2,1)} %tokens_hbm.1, bf16[576,1536]{1,0:T(8,128)(2,1)} %bitcast.10, bf16[192,1536]{1,0:T(8,128)(2,1)} %vit_out_hbm.1, bf16[12,128]{1,0:T(8,128)(2,1)} %bitcast.11, bf16[1536,768]{1,0:T(8,128)(2,1)} %fresh_proj_hbm.1, s32[1,256]{1,0:T(1,128)} %bitcast.13, ...), custom_call_target="tpu_custom_call" | custom-call | tf_op jit(solution)/shard_map/pallas_call | solution.py:623
  79.0 1.6 %copy.14 = bf16[128,768]{1,0:T(8,128)(2,1)} copy(bf16[128,768]{1,0:T(8,128)(2,1)} %shard_map.118) | data formatting | bytes 393216
where the time goes:
time: 80.8 us; the launch traced here: 80.6 us
  Pallas kernels  79 us (98%)
  local copies, waits for them, and re-layouts  1.62 us (2%)
    pallas_call x1, Pallas kernels, whole_layer(): pl.pallas_call(whole_kernel, out_shape=jax.ShapeDtypeStruct((ROWS, LD), B...  79 us
    unnamed x1, local copies, waits for them, and re-layouts  1.62 us

commit v1 on v0

--- a/solution.py
+++ b/solution.py
@@ -32,7 +32,8 @@
 SEG = 1024
 CHUNK = 2048
 KX = 64
-GROUP = 2
+FAR = 1536
+GROUP = 4
 WIDE = GROUP * TOK
 AHEAD = 4
 VIT_SCALE = LOG2E / math.sqrt(VS)
@@ -63,10 +64,6 @@
 def whole_row(ref):
     rows = ref[...].astype(F32)
     return jnp.concatenate([rows[k : k + 1] for k in range(rows.shape[0])], axis=1)
-
-
-def bit_reversed(rank):
-    return (rank % 2) * 8 + (rank // 2 % 2) * 4 + (rank // 4 % 2) * 2 + rank // 8
 
 
 def whole_kernel(
@@ -106,6 +103,7 @@
     same,
     lands,
     keep,
+    far_marks,
     packed,
     qkv,
     perm,
@@ -143,6 +141,8 @@
             device_id_type=MESH,
         )
 
+    half_lanes = pl.ds(pl.multiple_of(t % 2 * (LD // 2), LD // 2), LD // 2)
+
     def tile_rows(index):
         return pl.ds(pl.multiple_of(index * 16, 16), 16)
 
@@ -187,8 +187,12 @@
         return remote(65 + k, fresh_in.at[t], fresh_in.at[t], (d, (t + k) % 8))
 
     def spread_copy(k):
-        slot = fresh_all.at[tile_rows(d)]
+        slot = fresh_all.at[tile_rows(d), half_lanes]
         return remote(72 + k, slot, slot, ((d + k) % 16, t))
+
+    def sibling_copy(k):
+        slot = fresh_all.at[:, half_lanes]
+        return remote(102 + k, slot, slot, (d, t + 1 - 2 * (t % 2)))
 
     def mix_copy(k):
         device = (mine + k) % 16
@@ -234,44 +238,49 @@
     col = iota((16, D), 1)
     extra = jnp.where(row == 0, 1.0, jnp.where((row == 1) & (col == 0), 1.0, 0.0))
     vit_qkv[VW : VW + 16, :] = extra.astype(BF16)
-    shift = head_shift_ref[mine] % 16
-    place = iota((SEG, 1), 0)
-    goal = bit_reversed((place + 16 - shift) % 16) * 64 + place // 16
-    perm[...] = jnp.where(goal == iota((SEG, SEG), 1), 1.0, 0.0).astype(BF16)
+    shift = head_shift_ref[mine] & 15
     end0 = slide_tiles_ref[0]
     end1 = end0 + slide_tiles_ref[1]
     end2 = end1 + slide_tiles_ref[2]
 
-    def slides(count, width, which):
-        lane = iota((16, count), 1)
-        spot = lane % width
-        row = (
-            SEG * (2 * which + lane // width)
-            + 16 * (spot % 64)
-            + (bit_reversed(spot // 64) + shift) % 16
-        )
-        return (
-            (row >= end0).astype(jnp.int32)
-            + (row >= end1).astype(jnp.int32)
-            + (row >= end2).astype(jnp.int32)
-        )
-
-    def query_marks(count, width, which):
-        ids = slides(count, width, which)
-        return jnp.where(ids == iota(ids.shape, 0), 1.0, 0.0).astype(BF16)
-
-    def key_marks(count, width, which):
-        ids = slides(count, width, which)
-        feature = iota(ids.shape, 0)
-        return jnp.where((feature < 4) & (ids != feature), OUTSIDE, 0.0).astype(BF16)
+    def picked_rows(count, bits, which):
+        lane = iota((1, count), 1)
+        spot = lane & ((1 << bits) - 1)
+        rank = spot >> 6
+        turned = ((rank & 1) << 3) | ((rank & 2) << 1) | ((rank & 4) >> 1) | ((rank & 8) >> 3)
+        inside = ((spot & 63) << 4) + ((turned + shift) & 15)
+        return SEG * (2 * which + (lane >> bits)) + inside
+
+    quad = chunk // 4
+    inner = chunk % 4
+    beside = chunk + 1 - 2 * (chunk % 2)
+    across = [quad * 4 + (1 - inner // 2) * 2 + (inner % 2 + k) % 2 for k in range(2)]
+    beyond = [(1 - quad) * 4 + (inner + 4 - k) % 4 for k in range(4)]
+    every_row = jnp.concatenate(
+        [picked_rows(CHUNK, 10, chunk), picked_rows(512, 8, beside)]
+        + [picked_rows(256, 7, which) for which in across]
+        + [picked_rows(128, 6, which) for which in beyond],
+        axis=1,
+    )
+    perm[...] = jnp.where(
+        iota((SEG, SEG), 0) == picked_rows(SEG, 10, 0), 1.0, 0.0
+    ).astype(BF16)
+    ids = (
+        (every_row >= end0).astype(jnp.int32)
+        + (every_row >= end1).astype(jnp.int32)
+        + (every_row >= end2).astype(jnp.int32)
+    )
+    feature = iota((16, CHUNK + FAR), 0)
+    own = ids[:, 0:CHUNK]
+    qx[LS:KX, :] = jnp.where(own == feature[:, 0:CHUNK], 1.0, 0.0).astype(BF16)
+    marks = jnp.where((feature < 4) & (ids != feature), OUTSIDE, 0.0).astype(BF16)
+    kx[LS:KX, :] = marks[:, 0:CHUNK]
+    far_marks[...] = marks[:, CHUNK:]
 
     def value_marks(count):
         return jnp.where(iota((16, count), 0) == 0, 1.0, 0.0).astype(BF16)
 
-    qx[LS:KX, :] = query_marks(CHUNK, SEG, chunk)
-    kx[LS:KX, :] = key_marks(CHUNK, SEG, chunk)
     vx[LS:KX, :] = value_marks(CHUNK)
-
 
     lane_target = target_ref[...]
     diagonal = iota((256, 256), 0) == iota((256, 256), 1)
@@ -282,28 +291,7 @@
     same[...] = jnp.where(equal, 1.0, 0.0).astype(BF16)
     earlier = jnp.where(equal & (iota((256, 256), 1) < iota((256, 256), 0)), 1.0, 0.0)
     leads = jnp.sum(earlier, axis=1, keepdims=True) < 0.5
-
-    def landing(which, width):
-        away = target - which * CHUNK
-        spot = away % SEG
-        lane = bit_reversed((spot + 16 - shift) % 16) * 64 + spot // 16
-        good = leads & (away >= 0) & (away < CHUNK) & (lane < width)
-        goal = jnp.where(good, away // SEG * width + lane, -1)
-        return jnp.where(goal == iota((256, 2 * width), 1), 1.0, 0.0).astype(BF16)
-
-    quad = chunk // 4
-    inner = chunk % 4
-    beside = chunk + 1 - 2 * (chunk % 2)
-    across = [quad * 4 + (1 - inner // 2) * 2 + (inner % 2 + k) % 2 for k in range(2)]
-    beyond = [(1 - quad) * 4 + (inner + 4 - k) % 4 for k in range(4)]
-    lands[:, 0:CHUNK] = landing(chunk, SEG)
-    lands[:, CHUNK : CHUNK + 512] = landing(beside, 256)
-    for k in range(2):
-        begin = CHUNK + 512 + 256 * k
-        lands[:, begin : begin + 256] = landing(across[k], 128)
-    for k in range(4):
-        begin = CHUNK + 1024 + 128 * k
-        lands[:, begin : begin + 128] = landing(beyond[k], 64)
+    lands[...] = jnp.where(jnp.where(leads, target, -1) == every_row, 1.0, 0.0).astype(BF16)
     keep[...] = 1.0 - dot(jnp.ones((16, 256), BF16), lands[:, 0:CHUNK])[0:8]
 
     loads[2].wait()
@@ -417,18 +405,15 @@
         @pl.when(group == 0)
         def _():
             send_heads()
+            sum_over_dp()
 
         @pl.when(group == 1)
         def _():
-            sum_over_dp()
+            sort_rows()
+            sum_over_tensor()
 
         @pl.when(group == 2)
         def _():
-            sort_rows()
-
-        @pl.when(group == 3)
-        def _():
-            sum_over_tensor()
             for i in (0, 1, 4):
                 loads[i].start()
 
@@ -443,9 +428,8 @@
     pooled_term = dot(picks, attended[...], NT)
 
     loads[0].wait()
-    high, middle, low = split3(pooled_term)
-    weight = vit_out[...]
-    partial = dot(high, weight) + dot(middle, weight) + dot(low, weight)
+    partial = dot(jnp.concatenate(split3(pooled_term), axis=0), vit_out[...])
+    partial = partial[0:16] + partial[16:32] + partial[32:48]
     for k in range(8):
         part[k] = partial[2 * k : 2 * k + 2]
     every(reduce_copy, 7, "start")
@@ -462,11 +446,15 @@
     every(gather_copy, 7, "start")
     every(gather_copy, 7, "wait_recv")
     group = jnp.concatenate([fresh_in[k] for k in range(8)], axis=0).astype(BF16)
-    fresh_all[tile_rows(d)] = group
+    fresh_all[tile_rows(d), half_lanes] = jnp.where(
+        t % 2 == 0, group[:, 0 : LD // 2], group[:, LD // 2 : LD]
+    )
     every(spread_copy, 15, "start")
     every(last_copy, 15, "wait_recv")
     every(far_copy, 7, "wait_recv")
     every(spread_copy, 15, "wait_recv")
+    every(sibling_copy, 1, "start")
+    every(sibling_copy, 1, "wait_recv")
 
     changed = named_all[...].astype(F32) + dot(same[...], fresh_all[...])
     changed = (normalize_rows(changed) * whole_row(long_gain_ref)).astype(BF16)
@@ -481,16 +469,20 @@
     add(qx, slice(0, LS), everything, change[0:LS])
     add(kx, slice(0, LS), everything, change[LS : 2 * LS])
     add(vx, slice(0, LS), everything, change[2 * LS : LW])
-    far_change = dot(renewed[LS:LW], lands[:, CHUNK : CHUNK + 1536])
+    far_change = dot(renewed[LS:LW], lands[:, CHUNK : CHUNK + FAR])
     for side in range(2):
         lanes = slice(side * SEG, (side + 1) * SEG)
         keys_by_row[lanes, :] = jnp.transpose(kx[:, lanes])
 
-    def attend(keys, values, queries):
-        scores = dot(keys, queries)
-        highest = jnp.max(scores, axis=0, keepdims=True)
-        weights = jnp.exp2((scores - highest) * LONG_SCALE).astype(BF16)
-        return dot(values, weights), highest
+    def attend(jobs):
+        scores = [dot(keys, queries) for keys, _, queries in jobs]
+        highest = [jnp.max(score, axis=0, keepdims=True) for score in scores]
+        weights = [
+            jnp.exp2((score - high) * LONG_SCALE).astype(BF16)
+            for score, high in zip(scores, highest)
+        ]
+        results = [dot(values, weight) for (_, values, _), weight in zip(jobs, weights)]
+        return list(zip(results, highest))
 
     def merge(lanes, other_num, other_top):
         old_top = top[0:1, lanes]
@@ -501,15 +493,19 @@
         top[0:1, lanes] = new_top
 
     def first_pair(i, carry):
+        jobs = []
+        spots = []
         for side in range(2):
             lanes = slice(side * SEG, (side + 1) * SEG)
-            spot = pl.ds(pl.multiple_of(side * SEG + i * 256, 256), 256)
-            result, highest = attend(keys_by_row[lanes, :], vx[:, lanes], qx[:, spot])
+            spot = pl.ds(pl.multiple_of(side * SEG + i * 512, 512), 512)
+            jobs.append((keys_by_row[lanes, :], vx[:, lanes], qx[:, spot]))
+            spots.append(spot)
+        for spot, (result, highest) in zip(spots, attend(jobs)):
             num[:, spot] = result
             top[0:1, spot] = highest
         return carry
 
-    lax.fori_loop(0, 4, first_pair, 0)
+    lax.fori_loop(0, 2, first_pair, 0)
 
     def joined(ref, width):
         return jnp.concatenate([ref[:, 0:width], ref[:, SEG : SEG + width]], axis=1)
@@ -517,40 +513,31 @@
     def joined_rows(width):
         return [keys_by_row[0:width, :], keys_by_row[SEG : SEG + width, :]]
 
-    def second_pair(i, carry):
-        keys = jnp.concatenate(joined_rows(512), axis=0)
-        values = joined(vx, 512)
-        for side in range(2):
-            spot = pl.ds(pl.multiple_of(side * SEG + i * 256, 256), 256)
-            merge(spot, *attend(keys, values, qx[:, spot]))
-        return carry
-
-    lax.fori_loop(0, 2, second_pair, 0)
-
-    def arrived(block, begin, count, width, which):
-        block = (block.astype(F32) + far_change[:, begin : begin + count]).astype(BF16)
-        key = jnp.concatenate([block[0:LS], key_marks(count, width, which)], axis=0)
+    keys = jnp.concatenate(joined_rows(512), axis=0)
+    values = joined(vx, 512)
+    jobs = [(keys, values, qx[:, side * SEG : side * SEG + 512]) for side in range(2)]
+
+    def arrived(block, begin, count):
+        place = slice(begin, begin + count)
+        block = (block.astype(F32) + far_change[:, place]).astype(BF16)
+        key = jnp.concatenate([block[0:LS], far_marks[:, place]], axis=0)
         value = jnp.concatenate([block[LS : 2 * LS], value_marks(count)], axis=0)
         return jnp.transpose(key), value
 
-    key2, value2 = arrived(got2[...], 0, 512, 256, beside)
+    key2, value2 = arrived(got2[...], 0, 512)
     keys = jnp.concatenate(joined_rows(256) + [key2], axis=0)
     values = jnp.concatenate([joined(vx, 256), value2], axis=1)
-    for side in range(2):
-        lanes = slice(side * SEG, side * SEG + 256)
-        merge(lanes, *attend(keys, values, qx[:, lanes]))
+    jobs.append((keys, values, joined(qx, 256)))
 
     keys3 = joined_rows(128) + [key2[0:128], key2[256:384]]
     values3 = [joined(vx, 128), value2[:, 0:128], value2[:, 256:384]]
     for k in range(2):
-        key, value = arrived(got3[k], 512 + 256 * k, 256, 128, across[k])
+        key, value = arrived(got3[k], 512 + 256 * k, 256)
         keys3 += [key[0:128], key[128:256]]
         values3.append(value)
     keys = jnp.concatenate(keys3, axis=0)
     values = jnp.concatenate(values3, axis=1)
-    result, highest = attend(keys, values, joined(qx, 128))
-    merge(slice(0, 128), result[:, 0:128], highest[:, 0:128])
-    merge(slice(SEG, SEG + 128), result[:, 128:256], highest[:, 128:256])
+    jobs.append((keys, values, joined(qx, 128)))
 
     lower = iota((KX, 128), 1) < 64
 
@@ -567,13 +554,23 @@
     for far in values3[3:]:
         values4.append(packed_pair(far[:, 0:128], far[:, 128:256]))
     for k in range(4):
-        key, value = arrived(got4[k], 1024 + 128 * k, 128, 64, beyond[k])
+        key, value = arrived(got4[k], 1024 + 128 * k, 128)
         keys4.append(key)
         values4.append(value)
     keys = jnp.concatenate(keys4, axis=0)
     values = jnp.concatenate(values4, axis=1)
     query = packed_pair(qx[:, 0:128], qx[:, SEG : SEG + 128])
-    result, highest = attend(keys, values, query)
+    jobs.append((keys, values, query))
+    done = attend(jobs)
+    for side in range(2):
+        merge(slice(side * SEG, side * SEG + 512), *done[side])
+    for (result, highest), width in ((done[2], 256), (done[3], 128)):
+        for side in range(2):
+            lanes = slice(side * width, (side + 1) * width)
+            merge(
+                slice(side * SEG, side * SEG + width), result[:, lanes], highest[:, lanes]
+            )
+    result, highest = done[4]
     highest = jnp.broadcast_to(highest, (8, 128))
     for side in range(2):
         if side == 1:
@@ -588,7 +585,7 @@
 
     for side in range(2):
         lanes = slice(side * SEG, (side + 1) * SEG)
-        blended = (num[0:LS, lanes] / num[LS : LS + 1, lanes]).astype(BF16)
+        blended = (num[0:LS, lanes] * (1.0 / num[LS : LS + 1, lanes])).astype(BF16)
         natural = dot(blended, perm[...], NT).astype(BF16)
         for i in range(8):
             mix_out[side * 8 + i] = natural[:, i * ROWS : (i + 1) * ROWS]
@@ -611,6 +608,7 @@
         (reduce_copy, 7),
         (gather_copy, 7),
         (spread_copy, 15),
+        (sibling_copy, 1),
         (mix_copy, 15),
     ):
         every(copy, count, "wait_send")
@@ -647,8 +645,9 @@
             pltpu.VMEM((128, LD), BF16),
             pltpu.VMEM((256, LD), BF16),
             pltpu.VMEM((256, 256), BF16),
-            pltpu.VMEM((256, CHUNK + 1536), BF16),
+            pltpu.VMEM((256, CHUNK + FAR), BF16),
             pltpu.VMEM((8, CHUNK), F32),
+            pltpu.VMEM((16, FAR), BF16),
             pltpu.VMEM((15, LW, ROWS), BF16),
             pltpu.VMEM((LW, CHUNK), BF16),
             pltpu.VMEM((SEG, SEG), BF16),
@@ -668,7 +667,7 @@
             pltpu.VMEM((16, LS, ROWS), BF16),
             pltpu.SemaphoreType.DMA((TILES_HERE,)),
             pltpu.SemaphoreType.DMA((6,)),
-            pltpu.SemaphoreType.DMA((2, 103)),
+            pltpu.SemaphoreType.DMA((2, 104)),
         ],
         compiler_params=pltpu.CompilerParams(
             collective_id=0,

time: 80.8 us -> 69 us (0.85)
  Pallas kernels: 79 us -> 67.2 us
    pallas_call x1, Pallas kernels: 79 us -> 67.2 us  [whole_layer(): pl.pallas_call(whole_kernel, out_shape=jax.ShapeDtypeStruct((ROWS, LD), B...]
where the time goes in v1:
time: 69 us; the launch traced here: 68.9 us
  Pallas kernels  67.2 us (97%)
  local copies, waits for them, and re-layouts  1.62 us (2%)
    pallas_call x1, Pallas kernels, whole_layer(): pl.pallas_call(whole_kernel, out_shape=jax.ShapeDtypeStruct((ROWS, LD), B...  67.2 us
    unnamed x1, local copies, waits for them, and re-layouts  1.62 us

profile of v1, /device:TPU:1, one launch (start us, length us, event | category | flops | bytes accessed | tf_op | source)
XLA Modules:
  0.0 68.9 jit_solution(6426429667267168888)
XLA Ops:
  0.0 67.2 %shard_map.118 = bf16[128,768]{1,0:T(8,128)(2,1)} custom-call(bf16[16,256,1536]{2,1,0:T(8,128)(2,1)} %tokens_hbm.1, bf16[576,1536]{1,0:T(8,128)(2,1)} %bitcast.10, bf16[192,1536]{1,0:T(8,128)(2,1)} %vit_out_hbm.1, bf16[12,128]{1,0:T(8,128)(2,1)} %bitcast.11, bf16[1536,768]{1,0:T(8,128)(2,1)} %fresh_proj_hbm.1, s32[1,256]{1,0:T(1,128)} %bitcast.13, ...), custom_call_target="tpu_custom_call" | custom-call | tf_op jit(solution)/shard_map/pallas_call | solution.py:621
  67.2 1.6 %copy.14 = bf16[128,768]{1,0:T(8,128)(2,1)} copy(bf16[128,768]{1,0:T(8,128)(2,1)} %shard_map.118) | data formatting | bytes 393216

commit v2 on v1

--- a/solution.py
+++ b/solution.py
@@ -152,53 +152,68 @@
     def named_copy(k):
         peer = (d + k) % 16
         return remote(
-            k - 1, named_out.at[tile_rows(peer)], named_in.at[tile_rows(d)], (peer, t)
+            0, named_out.at[tile_rows(peer)], named_in.at[tile_rows(d)], (peer, t)
         )
 
     def middle_copy(k):
         slot = named_mid.at[tile_rows(t)]
-        return remote(14 + k, slot, slot, (d, (t + k) % 8))
+        return remote(1, slot, slot, (d, (t + k) % 8))
 
     def last_copy(k):
         slot = named_all.at[tile_rows(d)]
-        return remote(21 + k, slot, slot, ((d + k) % 16, t))
+        return remote(2, slot, slot, ((d + k) % 16, t))
 
     def head_copy(k):
         lanes = pl.ds(pl.multiple_of(mine * ROWS, ROWS), ROWS)
-        return remote(
-            36 + k, packed.at[k - 1], qkv.at[:, lanes], chunk_device((mine + k) % 16)
-        )
+        head = (mine + k) % 16
+        return remote(3, packed.at[head], qkv.at[:, lanes], chunk_device(head))
 
     def far_copy(k):
         quad, inner = chunk // 4, chunk % 4
         if k == 0:
-            return remote(52, send2, got2, (2 * (chunk + 1 - 2 * (chunk % 2)) + half, t))
+            return remote(9, send2, got2, (2 * (chunk + 1 - 2 * (chunk % 2)) + half, t))
         if k < 3:
             other = quad * 4 + (1 - inner // 2) * 2 + (inner % 2 + k - 1) % 2
-            return remote(52 + k, send3, got3.at[k - 1], (2 * other + half, t))
+            return remote(9 + k, send3, got3.at[k - 1], (2 * other + half, t))
         other = (1 - quad) * 4 + (inner + k - 3) % 4
-        return remote(52 + k, send4, got4.at[k - 3], (2 * other + half, t))
+        return remote(9 + k, send4, got4.at[k - 3], (2 * other + half, t))
 
     def reduce_copy(k):
         peer = (t + k) % 8
-        return remote(58 + k, part.at[peer], part_in.at[t], (d, peer))
+        return remote(4, part.at[peer], part_in.at[t], (d, peer))
 
     def gather_copy(k):
-        return remote(65 + k, fresh_in.at[t], fresh_in.at[t], (d, (t + k) % 8))
+        return remote(5, fresh_in.at[t], fresh_in.at[t], (d, (t + k) % 8))
 
     def spread_copy(k):
         slot = fresh_all.at[tile_rows(d), half_lanes]
-        return remote(72 + k, slot, slot, ((d + k) % 16, t))
+        return remote(6, slot, slot, ((d + k) % 16, t))
 
     def sibling_copy(k):
         slot = fresh_all.at[:, half_lanes]
-        return remote(102 + k, slot, slot, (d, t + 1 - 2 * (t % 2)))
+        return remote(7, slot, slot, (d, t + 1 - 2 * (t % 2)))
 
     def mix_copy(k):
         device = (mine + k) % 16
-        return remote(87 + k, mix_out.at[device], mix_in.at[mine], chunk_device(device))
+        return remote(8, mix_out.at[device], mix_in.at[mine], chunk_device(device))
+
+    whole = {
+        named_copy: (0, named_out.at[0:240]),
+        middle_copy: (1, named_mid.at[0:112]),
+        last_copy: (2, named_all.at[0:240]),
+        head_copy: (3, packed.at[0:15]),
+        reduce_copy: (4, part.at[0:7]),
+        gather_copy: (5, fresh_in.at[0:7]),
+        spread_copy: (6, fresh_all.at[0:240, half_lanes]),
+        sibling_copy: (7, fresh_all.at[:, half_lanes]),
+        mix_copy: (8, mix_out.at[0:15]),
+    }
 
     def every(copy, count, what):
+        if what != "start" and copy in whole:
+            i, total = whole[copy]
+            getattr(remote(i, total, total, (d, (t + 1) % 8)), what)()
+            return
         first = 0 if copy is far_copy else 1
         for k in range(first, first + count):
             getattr(copy(k), what)()
@@ -232,7 +247,6 @@
 
     for i in range(AHEAD):
         token_load(i).start()
-    loads[3].start()
 
     row = iota((16, D), 0)
     col = iota((16, D), 1)
@@ -316,28 +330,21 @@
         named_all[tile_rows(d)] = total.astype(BF16)
         every(last_copy, 15, "start")
 
-    def head_block(head):
-        weight = long_qkv[pl.ds(pl.multiple_of(head * LW, LW), LW), :]
-        return dot(weight, hidden[...], NT).astype(BF16)
-
     def send_heads():
         loads[3].wait()
-
-        def send_head(k, carry):
-            packed[k - 1] = head_block((mine + k) % 16)
-            head_copy(k).start()
-            return carry
-
-        lax.fori_loop(1, 16, send_head, 0)
-        qkv[:, pl.ds(pl.multiple_of(mine * ROWS, ROWS), ROWS)] = head_block(mine)
+        packed[...] = dot(long_qkv[...], hidden[...], NT).astype(BF16).reshape(LH, LW, ROWS)
+        every(head_copy, 15, "start")
+        qkv[:, pl.ds(pl.multiple_of(mine * ROWS, ROWS), ROWS)] = packed[mine]
 
     def sort_rows():
         every(head_copy, 15, "wait_recv")
         low_half = iota((LW, 128), 1) < 64
+        stacked = jnp.concatenate([qkv[:, 0:SEG], qkv[:, SEG:CHUNK]], axis=0)
+        stacked = dot(stacked, perm[...])
         sides = []
         for side in range(2):
             lanes = slice(side * SEG, (side + 1) * SEG)
-            ordered = dot(qkv[:, lanes], perm[...]) * keep[0:1, lanes]
+            ordered = stacked[side * LW : (side + 1) * LW] * keep[0:1, lanes]
             sides.append(ordered[:, 0:128])
             ordered = ordered.astype(BF16)
             qx[0:LS, lanes] = ordered[0:LS]
@@ -361,6 +368,10 @@
             @pl.when(after < TILES_HERE)
             def _():
                 token_load(after).start()
+
+        @pl.when(group == 0)
+        def _():
+            loads[3].start()
 
         x = tokens[pl.ds(group * GROUP, GROUP)].reshape(WIDE, D)
         raw = dot(vit_qkv[...], x, NT)
@@ -583,12 +594,16 @@
             jnp.where(lower[0:1], highest[0:1], OUTSIDE),
         )
 
+    blended = []
     for side in range(2):
         lanes = slice(side * SEG, (side + 1) * SEG)
-        blended = (num[0:LS, lanes] * (1.0 / num[LS : LS + 1, lanes])).astype(BF16)
-        natural = dot(blended, perm[...], NT).astype(BF16)
+        blended.append((num[0:LS, lanes] * (1.0 / num[LS : LS + 1, lanes])).astype(BF16))
+    natural = dot(jnp.concatenate(blended, axis=0), perm[...], NT).astype(BF16)
+    for side in range(2):
         for i in range(8):
-            mix_out[side * 8 + i] = natural[:, i * ROWS : (i + 1) * ROWS]
+            mix_out[side * 8 + i] = natural[
+                side * LS : (side + 1) * LS, i * ROWS : (i + 1) * ROWS
+            ]
     every(mix_copy, 15, "start")
     mix_in[pl.ds(mine, 1)] = mix_out[pl.ds(mine, 1)]
     match = (lane_target - first_row == iota((ROWS, 256), 0))
@@ -648,7 +663,7 @@
             pltpu.VMEM((256, CHUNK + FAR), BF16),
             pltpu.VMEM((8, CHUNK), F32),
             pltpu.VMEM((16, FAR), BF16),
-            pltpu.VMEM((15, LW, ROWS), BF16),
+            pltpu.VMEM((16, LW, ROWS), BF16),
             pltpu.VMEM((LW, CHUNK), BF16),
             pltpu.VMEM((SEG, SEG), BF16),
             pltpu.VMEM((KX, CHUNK), BF16),
@@ -667,7 +682,7 @@
             pltpu.VMEM((16, LS, ROWS), BF16),
             pltpu.SemaphoreType.DMA((TILES_HERE,)),
             pltpu.SemaphoreType.DMA((6,)),
-            pltpu.SemaphoreType.DMA((2, 104)),
+            pltpu.SemaphoreType.DMA((2, 16)),
         ],
         compiler_params=pltpu.CompilerParams(
             collective_id=0,

time: 69 us -> 67 us (0.971)
  Pallas kernels: 67.2 us -> 65.2 us
    pallas_call x1, Pallas kernels: 67.2 us -> 65.2 us  [whole_layer(): pl.pallas_call(whole_kernel, out_shape=jax.ShapeDtypeStruct((ROWS, LD), B...]
where the time goes in v2:
time: 67 us; the launch traced here: 66.8 us
  Pallas kernels  65.2 us (97%)
  local copies, waits for them, and re-layouts  1.62 us (2%)
    pallas_call x1, Pallas kernels, whole_layer(): pl.pallas_call(whole_kernel, out_shape=jax.ShapeDtypeStruct((ROWS, LD), B...  65.2 us
    unnamed x1, local copies, waits for them, and re-layouts  1.62 us

profile of v2, /device:TPU:1, one launch (start us, length us, event | category | flops | bytes accessed | tf_op | source)
XLA Modules:
  0.0 66.8 jit_solution(1143236042801131600)
XLA Ops:
  0.0 65.2 %shard_map.118 = bf16[128,768]{1,0:T(8,128)(2,1)} custom-call(bf16[16,256,1536]{2,1,0:T(8,128)(2,1)} %tokens_hbm.1, bf16[576,1536]{1,0:T(8,128)(2,1)} %bitcast.10, bf16[192,1536]{1,0:T(8,128)(2,1)} %vit_out_hbm.1, bf16[12,128]{1,0:T(8,128)(2,1)} %bitcast.11, bf16[1536,768]{1,0:T(8,128)(2,1)} %fresh_proj_hbm.1, s32[1,256]{1,0:T(1,128)} %bitcast.13, ...), custom_call_target="tpu_custom_call" | custom-call | tf_op jit(solution)/shard_map/pallas_call | solution.py:636
  65.2 1.6 %copy.14 = bf16[128,768]{1,0:T(8,128)(2,1)} copy(bf16[128,768]{1,0:T(8,128)(2,1)} %shard_map.118) | data formatting | bytes 393216

commit v3 on v2

--- a/solution.py
+++ b/solution.py
@@ -420,13 +420,13 @@
 
         @pl.when(group == 1)
         def _():
-            sort_rows()
             sum_over_tensor()
+            for i in (0, 1, 4):
+                loads[i].start()
 
         @pl.when(group == 2)
         def _():
-            for i in (0, 1, 4):
-                loads[i].start()
+            sort_rows()
 
         return carry
 

time: 67 us -> 67.8 us (1.012)
  Pallas kernels: 65.2 us -> 66 us
    pallas_call x1, Pallas kernels: 65.2 us -> 66 us  [whole_layer(): pl.pallas_call(whole_kernel, out_shape=jax.ShapeDtypeStruct((ROWS, LD), B...]
where the time goes in v3:
time: 67.8 us; the launch traced here: 67.6 us
  Pallas kernels  66 us (97%)
  local copies, waits for them, and re-layouts  1.62 us (2%)
    pallas_call x1, Pallas kernels, whole_layer(): pl.pallas_call(whole_kernel, out_shape=jax.ShapeDtypeStruct((ROWS, LD), B...  66 us
    unnamed x1, local copies, waits for them, and re-layouts  1.62 us

profile of v3, /device:TPU:1, one launch (start us, length us, event | category | flops | bytes accessed | tf_op | source)
XLA Modules:
  0.0 67.6 jit_solution(6459550493945380908)
XLA Ops:
  0.0 66.0 %shard_map.118 = bf16[128,768]{1,0:T(8,128)(2,1)} custom-call(bf16[16,256,1536]{2,1,0:T(8,128)(2,1)} %tokens_hbm.1, bf16[576,1536]{1,0:T(8,128)(2,1)} %bitcast.10, bf16[192,1536]{1,0:T(8,128)(2,1)} %vit_out_hbm.1, bf16[12,128]{1,0:T(8,128)(2,1)} %bitcast.11, bf16[1536,768]{1,0:T(8,128)(2,1)} %fresh_proj_hbm.1, s32[1,256]{1,0:T(1,128)} %bitcast.13, ...), custom_call_target="tpu_custom_call" | custom-call | tf_op jit(solution)/shard_map/pallas_call | solution.py:636
  66.0 1.6 %copy.14 = bf16[128,768]{1,0:T(8,128)(2,1)} copy(bf16[128,768]{1,0:T(8,128)(2,1)} %shard_map.118) | data formatting | bytes 393216

commit v4 on v2

--- a/solution.py
+++ b/solution.py
@@ -431,9 +431,6 @@
         return carry
 
     lax.fori_loop(0, groups, one_group, 0)
-    for i in range(2):
-        sums = dot(jnp.ones((16, TOK), BF16), tokens[2 * t + i])
-        token_mean[i : i + 1, :] = sums[0:1] * (1.0 / TOK)
     tile_of = iota((TILES_HERE, TILES_HERE * TOK), 1) // TOK
     picks = jnp.where(iota(tile_of.shape, 0) == tile_of, 1.0 / TOK, 0.0).astype(BF16)
     pooled_term = dot(picks, attended[...], NT)
@@ -445,6 +442,9 @@
         part[k] = partial[2 * k : 2 * k + 2]
     every(reduce_copy, 7, "start")
     part_in[pl.ds(t, 1)] = part[pl.ds(t, 1)]
+    for i in range(2):
+        sums = dot(jnp.ones((16, TOK), BF16), tokens[2 * t + i])
+        token_mean[i : i + 1, :] = sums[0:1] * (1.0 / TOK)
 
     every(reduce_copy, 7, "wait_recv")
     pooled = token_mean[0:2, :]

time: 67 us -> 66.6 us (level)
  no operation moved by 1% of the time
where the time goes in v4:
time: 66.6 us; the launch traced here: 66.4 us
  Pallas kernels  64.8 us (97%)
  local copies, waits for them, and re-layouts  1.62 us (2%)
    pallas_call x1, Pallas kernels, whole_layer(): pl.pallas_call(whole_kernel, out_shape=jax.ShapeDtypeStruct((ROWS, LD), B...  64.8 us
    unnamed x1, local copies, waits for them, and re-layouts  1.62 us

profile of v4, /device:TPU:1, one launch (start us, length us, event | category | flops | bytes accessed | tf_op | source)
XLA Modules:
  0.0 66.4 jit_solution(2225057369591739853)
XLA Ops:
  0.0 64.8 %shard_map.118 = bf16[128,768]{1,0:T(8,128)(2,1)} custom-call(bf16[16,256,1536]{2,1,0:T(8,128)(2,1)} %tokens_hbm.1, bf16[576,1536]{1,0:T(8,128)(2,1)} %bitcast.10, bf16[192,1536]{1,0:T(8,128)(2,1)} %vit_out_hbm.1, bf16[12,128]{1,0:T(8,128)(2,1)} %bitcast.11, bf16[1536,768]{1,0:T(8,128)(2,1)} %fresh_proj_hbm.1, s32[1,256]{1,0:T(1,128)} %bitcast.13, ...), custom_call_target="tpu_custom_call" | custom-call | tf_op jit(solution)/shard_map/pallas_call | solution.py:636
  64.8 1.6 %copy.14 = bf16[128,768]{1,0:T(8,128)(2,1)} copy(bf16[128,768]{1,0:T(8,128)(2,1)} %shard_map.118) | data formatting | bytes 393216

commit v5 on v4

--- a/solution.py
+++ b/solution.py
@@ -314,9 +314,10 @@
     hidden[...] = (normalize_rows(stored.astype(F32)) * whole_row(long_gain_ref)).astype(BF16)
     mine_only = jnp.where(target - first_row == iota((256, ROWS), 1), 1.0, 0.0).astype(BF16)
     named_out[...] = dot(mine_only, stored).astype(BF16)
-    pl.semaphore_wait(barrier, 29)
-    every(named_copy, 15, "start")
-    named_in[tile_rows(d)] = named_out[tile_rows(d)]
+    def greet():
+        pl.semaphore_wait(barrier, 29)
+        every(named_copy, 15, "start")
+        named_in[tile_rows(d)] = named_out[tile_rows(d)]
 
     def sum_over_dp():
         every(named_copy, 15, "wait_recv")
@@ -415,18 +416,19 @@
 
         @pl.when(group == 0)
         def _():
+            greet()
             send_heads()
-            sum_over_dp()
 
         @pl.when(group == 1)
         def _():
-            sort_rows()
-            sum_over_tensor()
+            sum_over_dp()
+            for i in (0, 1, 4):
+                loads[i].start()
 
         @pl.when(group == 2)
         def _():
-            for i in (0, 1, 4):
-                loads[i].start()
+            sum_over_tensor()
+            sort_rows()
 
         return carry
 

time: 66.6 us -> 67.9 us (1.020)
  Pallas kernels: 64.8 us -> 66.2 us
    pallas_call x1, Pallas kernels: 64.8 us -> 66.2 us  [whole_layer(): pl.pallas_call(whole_kernel, out_shape=jax.ShapeDtypeStruct((ROWS, LD), B...]
where the time goes in v5:
time: 67.9 us; the launch traced here: 67.8 us
  Pallas kernels  66.2 us (97%)
  local copies, waits for them, and re-layouts  1.62 us (2%)
    pallas_call x1, Pallas kernels, whole_layer(): pl.pallas_call(whole_kernel, out_shape=jax.ShapeDtypeStruct((ROWS, LD), B...  66.2 us
    unnamed x1, local copies, waits for them, and re-layouts  1.62 us

profile of v5, /device:TPU:1, one launch (start us, length us, event | category | flops | bytes accessed | tf_op | source)
XLA Modules:
  0.0 67.8 jit_solution(10800222340054038187)
XLA Ops:
  0.0 66.2 %shard_map.118 = bf16[128,768]{1,0:T(8,128)(2,1)} custom-call(bf16[16,256,1536]{2,1,0:T(8,128)(2,1)} %tokens_hbm.1, bf16[576,1536]{1,0:T(8,128)(2,1)} %bitcast.10, bf16[192,1536]{1,0:T(8,128)(2,1)} %vit_out_hbm.1, bf16[12,128]{1,0:T(8,128)(2,1)} %bitcast.11, bf16[1536,768]{1,0:T(8,128)(2,1)} %fresh_proj_hbm.1, s32[1,256]{1,0:T(1,128)} %bitcast.13, ...), custom_call_target="tpu_custom_call" | custom-call | tf_op jit(solution)/shard_map/pallas_call | solution.py:638
  66.2 1.6 %copy.14 = bf16[128,768]{1,0:T(8,128)(2,1)} copy(bf16[128,768]{1,0:T(8,128)(2,1)} %shard_map.118) | data formatting | bytes 393216
